TPU v7x, 32 devices: a whole 2x2x4 slice. The times are simulated.
32 devices in a mesh: alpha: 8 (over y, x, core), beta: 4 (over z).
Axes of the slice: x: 2, y: 2, z: 4, core: 2. Of those that a mesh axis runs over, the one named last changes fastest.
Arguments:
- coefficients: float32 [6144, 3072], P('alpha', 'beta'), may hold values from -6 to 6
- beta_blocks: float32 [8, 3, 384, 384], P('beta'), may hold values from -0.1875 to 0.1875
- alpha_blocks: float32 [16, 3, 384, 384], P('alpha'), may hold values from -0.1875 to 0.1875
- beta_links: int32 [8, 3], P('beta'), may hold values from 0 to 7, as said below
- alpha_links: int32 [16, 3], P('alpha'), may hold values from 0 to 15, as said below
- beta_count: int32 [8], P('beta'), may hold values from 1 to 3, as said below
- alpha_count: int32 [16], P('alpha'), may hold values from 1 to 3, as said below
Outputs:
- sigma_slab: float32 [6144, 3072], P('alpha', 'beta')
Inputs may be any that keep to these rules, and one draw needn't show every extreme that they name: `beta_links`: each row lists 3 distinct beta groups whose cyclic distance from the row's own group is at most 2. `alpha_links`: each row lists 3 distinct alpha groups whose cyclic distance from the row's own group is at most 2. `beta_count`: some group uses all 3 couplings. `alpha_count`: some group uses all 3 couplings.
All inputs are finite; a program needn't handle non-finite values.
Results may differ from a plain program's by a relative error of at most 0.0003.
Values sent between devices are 32-bit elements; how exact they have to be, the bound alone decides.
No kernel may reach another device: no remote copies, remote signals or barrier semaphores. Data moves between devices by JAX's collectives and lax.ppermute only.
A program may use at most 128 MiB of HBM per device.

v0:
```python
import jax
import jax.numpy as jnp
from jax import lax
from jax.sharding import PartitionSpec as P

G = 384
GPD = 2


def from_behind(block, axis, distance):
    devices = range(lax.axis_size(axis))
    route = [((i - distance) % len(devices), i) for i in devices]
    return lax.ppermute(block, axis, route)


def beta_section(stacked, blocks, links, count, my_index, owners):
    parts = []
    for local in range(GPD):

        def beta_accumulate(position, running, local=local):
            source = links[local, position]
            owner = source // GPD
            within = source % GPD
            slot = (owner - my_index + 1) % owners
            piece = lax.dynamic_index_in_dim(stacked, slot, 0, keepdims=False)
            columns = lax.dynamic_slice_in_dim(piece, within * G, G, 1)
            hblock = lax.dynamic_index_in_dim(blocks[local], position, 0, keepdims=False)
            return running + jnp.dot(
                columns, hblock, precision=lax.Precision.HIGHEST, preferred_element_type=jnp.float32
            )

        start = jnp.zeros((stacked.shape[1], G), jnp.float32)
        parts.append(lax.fori_loop(0, count[local], beta_accumulate, start))
    return jnp.concatenate(parts, axis=1)


def alpha_section(stacked, blocks, links, count, my_index, owners):
    parts = []
    for local in range(GPD):

        def alpha_accumulate(position, running, local=local):
            source = links[local, position]
            owner = source // GPD
            within = source % GPD
            slot = (owner - my_index + 1) % owners
            piece = lax.dynamic_index_in_dim(stacked, slot, 0, keepdims=False)
            rows = lax.dynamic_slice_in_dim(piece, within * G, G, 0)
            hblock = lax.dynamic_index_in_dim(blocks[local], position, 0, keepdims=False)
            return running + jnp.dot(
                hblock, rows, precision=lax.Precision.HIGHEST, preferred_element_type=jnp.float32
            )

        start = jnp.zeros((G, stacked.shape[2]), jnp.float32)
        parts.append(lax.fori_loop(0, count[local], alpha_accumulate, start))
    return jnp.concatenate(parts, axis=0)


def on_device(
    coefficients, beta_blocks, alpha_blocks, beta_links, alpha_links, beta_count, alpha_count
):
    beta_tiles = jnp.stack(
        [
            from_behind(coefficients, "beta", offset) if offset != 0 else coefficients
            for offset in (1, 0, -1)
        ]
    )
    alpha_tiles = jnp.stack(
        [
            from_behind(coefficients, "alpha", offset) if offset != 0 else coefficients
            for offset in (1, 0, -1)
        ]
    )
    beta_part = beta_section(
        beta_tiles,
        beta_blocks,
        beta_links,
        beta_count,
        lax.axis_index("beta"),
        lax.axis_size("beta"),
    )
    alpha_part = alpha_section(
        alpha_tiles,
        alpha_blocks,
        alpha_links,
        alpha_count,
        lax.axis_index("alpha"),
        lax.axis_size("alpha"),
    )
    return beta_part + alpha_part


def solution(mesh):
    in_specs = (
        P("alpha", "beta"),
        P("beta", None, None, None),
        P("alpha", None, None, None),
        P("beta", None),
        P("alpha", None),
        P("beta"),
        P("alpha"),
    )
    out_specs = P("alpha", "beta")
    return jax.shard_map(
        on_device, mesh=mesh, in_specs=in_specs, out_specs=out_specs, check_vma=False
    )
```

profile of v0, /device:TPU:22, one launch (start us, length us, event | category | flops | bytes accessed | tf_op | source)
XLA Modules:
  0.0 223.5 jit_solution(14720267022351334311)
XLA Ops:
  0.0 1.6 collective-permute-start
  1.6 0.4 collective-permute-start.1
  2.0 0.0 collective-permute-start.2
  2.0 1.7 collective-permute-start.3
  3.8 1.4 fusion.22
  5.1 1.4 fusion.23
  6.5 97.2 %collective-permute-done = f32[768,768]{1,0:T(8,128)S(1)} collective-permute-done((f32[768,768]{1,0:T(8,128)}, f32[768,768]{1,0:T(8,128)S(1)}, u32[]{:S(2)}, u32[]{:S(2)}) %collective-permute-start) | collective-permute-done | bytes 2359328 | tf_op jit(solution)/shard_map/ppermute | solution.py:13
  103.8 0.0 copy-start.1
  103.8 0.0 collective-permute-done.1
  103.8 0.0 collective-permute-done.2
  103.8 0.0 collective-permute-done.3
  103.8 1.4 copy-done.1
  105.2 0.0 copy-start
  105.2 0.0 copy-start.2
  105.2 9.2 %fusion.21 = (f32[3,768,768]{2,1,0:T(8,128)}, f32[3,768,768]{2,1,0:T(8,128)}) fusion(f32[1,768,768]{2,1,0:T(8,128)} %bitcast.61, f32[1,768,768]{2,1,0:T(8,128)} %bitcast.19, f32[1,768,768]{2,1,0:T(8,128)} %bitcast.18, f32[1,768,768]{2,1,0:T(8,128)} %bitcast.15, f32[1,768,768]{2,1,0:T(8,128)} %bitcast.62), kind=kLoop, calls=%fused_computation.31 | loop fusion | flops 7077888 | bytes 25952256 | tf_op jit(solution)/shard_map/stack | solution.py:67
  114.4 1.1 broadcast.19.clone.1
  115.5 0.0 copy-done
  115.5 0.0 copy-done.2
  115.5 27.1 %while.54 = (s32[]{:T(128)}, f32[384,768]{1,0:T(8,128)}, s32[]{:T(128)}, f32[2,3,384,384]{3,2,1,0:T(8,128)S(1)}, s32[2,3]{1,0:T(2,128)S(1)}, /*index=5*/s32[]{:T...) while((s32[]{:T(128)}, f32[384,768]{1,0:T(8,128)}, ...), condition=%wide.region_5.6_spmd, body=%wide.region_4.5_spmd.sunk | while | flops 1359249408 | bytes 7668351 | solution.py:54
  116.2 0.6 constant_dynamic-slice_fusion.10
  119.4 0.1 slice.54
  119.5 4.8 %convolution_add_fusion.10 = f32[384,768]{1,0:T(8,128)} fusion(f32[384,768]{1,0:T(8,128)} %get-tuple-element.926, f32[3,768,768]{2,1,0:T(8,128)} %get-tuple-element.947, s32[]{:T(128)S(6)} %select_n.270, s32[]{:T(128)S(6)} %select_n.273, f32[1,3,384,384]{3,2,1,0:T(8,128)S(1)} %slice.54, s32[]{:T(128)S(6)} %select_n.266), kind=kOutput, calls=%fused_computation.14.clone.1 | convolution fusion | flops 1359249408 | bytes 4128780 | tf_op jit(solution)/shard_map/while/body/dot_general | solution.py:49
  125.0 0.6 constant_dynamic-slice_fusion.10
  128.2 0.1 slice.54
  128.4 4.8 %convolution_add_fusion.10 = f32[384,768]{1,0:T(8,128)} fusion(f32[384,768]{1,0:T(8,128)} %get-tuple-element.926, f32[3,768,768]{2,1,0:T(8,128)} %get-tuple-element.947, s32[]{:T(128)S(6)} %select_n.270, s32[]{:T(128)S(6)} %select_n.273, f32[1,3,384,384]{3,2,1,0:T(8,128)S(1)} %slice.54, s32[]{:T(128)S(6)} %select_n.266), kind=kOutput, calls=%fused_computation.14.clone.1 | convolution fusion | flops 1359249408 | bytes 4128780 | tf_op jit(solution)/shard_map/while/body/dot_general | solution.py:49
  133.8 0.6 constant_dynamic-slice_fusion.10
  137.1 0.1 slice.54
  137.2 4.8 %convolution_add_fusion.10 = f32[384,768]{1,0:T(8,128)} fusion(f32[384,768]{1,0:T(8,128)} %get-tuple-element.926, f32[3,768,768]{2,1,0:T(8,128)} %get-tuple-element.947, s32[]{:T(128)S(6)} %select_n.270, s32[]{:T(128)S(6)} %select_n.273, f32[1,3,384,384]{3,2,1,0:T(8,128)S(1)} %slice.54, s32[]{:T(128)S(6)} %select_n.266), kind=kOutput, calls=%fused_computation.14.clone.1 | convolution fusion | flops 1359249408 | bytes 4128780 | tf_op jit(solution)/shard_map/while/body/dot_general | solution.py:49
  142.6 1.1 broadcast.19.clone
  143.7 0.0 copy-start.3
  143.7 26.9 %while.55 = (s32[]{:T(128)}, f32[384,768]{1,0:T(8,128)}, s32[]{:T(128)}, f32[2,3,384,384]{3,2,1,0:T(8,128)S(1)}, s32[2,3]{1,0:T(2,128)S(1)}, /*index=5*/s32[]{:T...) while((s32[]{:T(128)}, f32[384,768]{1,0:T(8,128)}, ...), condition=%wide.region_7.8_spmd, body=%wide.region_6.7_spmd.sunk | while | flops 1359249408 | bytes 7668351 | solution.py:54
  144.4 0.6 constant_dynamic-slice_fusion.11
  147.6 0.1 slice.55
  147.7 4.8 %convolution_add_fusion.11 = f32[384,768]{1,0:T(8,128)} fusion(f32[384,768]{1,0:T(8,128)} %get-tuple-element.878, f32[3,768,768]{2,1,0:T(8,128)} %get-tuple-element.899, s32[]{:T(128)S(6)} %select_n.278, s32[]{:T(128)S(6)} %select_n.281, f32[1,3,384,384]{3,2,1,0:T(8,128)S(1)} %slice.55, s32[]{:T(128)S(6)} %select_n.274), kind=kOutput, calls=%fused_computation.21.clone.1 | convolution fusion | flops 1359249408 | bytes 4128780 | tf_op jit(solution)/shard_map/while/body/dot_general | solution.py:49
  153.1 0.6 constant_dynamic-slice_fusion.11
  156.4 0.1 slice.55
  156.5 4.8 %convolution_add_fusion.11 = f32[384,768]{1,0:T(8,128)} fusion(f32[384,768]{1,0:T(8,128)} %get-tuple-element.878, f32[3,768,768]{2,1,0:T(8,128)} %get-tuple-element.899, s32[]{:T(128)S(6)} %select_n.278, s32[]{:T(128)S(6)} %select_n.281, f32[1,3,384,384]{3,2,1,0:T(8,128)S(1)} %slice.55, s32[]{:T(128)S(6)} %select_n.274), kind=kOutput, calls=%fused_computation.21.clone.1 | convolution fusion | flops 1359249408 | bytes 4128780 | tf_op jit(solution)/shard_map/while/body/dot_general | solution.py:49
  161.9 0.6 constant_dynamic-slice_fusion.11
  165.1 0.1 slice.55
  165.2 4.8 %convolution_add_fusion.11 = f32[384,768]{1,0:T(8,128)} fusion(f32[384,768]{1,0:T(8,128)} %get-tuple-element.878, f32[3,768,768]{2,1,0:T(8,128)} %get-tuple-element.899, s32[]{:T(128)S(6)} %select_n.278, s32[]{:T(128)S(6)} %select_n.281, f32[1,3,384,384]{3,2,1,0:T(8,128)S(1)} %slice.55, s32[]{:T(128)S(6)} %select_n.274), kind=kOutput, calls=%fused_computation.21.clone.1 | convolution fusion | flops 1359249408 | bytes 4128780 | tf_op jit(solution)/shard_map/while/body/dot_general | solution.py:49
  170.7 0.1 broadcast.18.clone.1
  170.7 0.0 copy-done.3
  170.7 19.7 %while.52 = (s32[]{:T(128)}, f32[768,384]{1,0:T(8,128)S(1)}, s32[]{:T(128)}, s32[2,3]{1,0:T(2,128)S(1)}, s32[]{:T(128)}, /*index=5*/f32[3,768,768]{2,1,0:T(8,128...) while((s32[]{:T(128)}, f32[768,384]{1,0:T(8,128)S(1)}, ...), condition=%wide.region_1.2_spmd, body=%wide.region_0.1_spmd.sunk | while | flops 1359249408 | bytes 7668343 | solution.py:33
  171.3 0.6 constant_dynamic-slice_fusion.8
  174.6 1.6 slice.52
  176.2 4.1 %convolution_add_fusion.8 = f32[768,384]{1,0:T(8,128)S(1)} fusion(f32[768,384]{1,0:T(8,128)S(1)} %get-tuple-element.832, f32[3,768,768]{2,1,0:T(8,128)} %get-tuple-element.851, s32[]{:T(128)S(6)} %select_n.254, s32[]{:T(128)S(6)} %select_n.257, f32[1,3,384,384]{3,2,1,0:T(8,128)S(1)} %slice.52, s32[]{:T(128)S(6)} %select_n.250), kind=kOutput, calls=%fused_computation.clone.1 | convolution fusion | flops 1359249408 | bytes 4128780 | tf_op jit(solution)/shard_map/while/body/dot_general | solution.py:28
  180.8 0.6 constant_dynamic-slice_fusion.8
  184.1 1.6 slice.52
  185.7 4.2 %convolution_add_fusion.8 = f32[768,384]{1,0:T(8,128)S(1)} fusion(f32[768,384]{1,0:T(8,128)S(1)} %get-tuple-element.832, f32[3,768,768]{2,1,0:T(8,128)} %get-tuple-element.851, s32[]{:T(128)S(6)} %select_n.254, s32[]{:T(128)S(6)} %select_n.257, f32[1,3,384,384]{3,2,1,0:T(8,128)S(1)} %slice.52, s32[]{:T(128)S(6)} %select_n.250), kind=kOutput, calls=%fused_computation.clone.1 | convolution fusion | flops 1359249408 | bytes 4128780 | tf_op jit(solution)/shard_map/while/body/dot_general | solution.py:28
  190.5 0.1 broadcast.18.clone
  190.6 29.7 %while.53 = (s32[]{:T(128)}, f32[768,384]{1,0:T(8,128)S(1)}, s32[]{:T(128)}, s32[2,3]{1,0:T(2,128)S(1)}, s32[]{:T(128)}, /*index=5*/f32[3,768,768]{2,1,0:T(8,128...) while((s32[]{:T(128)}, f32[768,384]{1,0:T(8,128)S(1)}, ...), condition=%wide.region_3.4_spmd, body=%wide.region_2.3_spmd.sunk | while | flops 1359249408 | bytes 7668343 | solution.py:33
  191.4 0.6 constant_dynamic-slice_fusion.9
  194.6 1.6 slice.53
  196.2 4.1 %convolution_add_fusion.9 = f32[768,384]{1,0:T(8,128)S(1)} fusion(f32[768,384]{1,0:T(8,128)S(1)} %get-tuple-element.787, f32[3,768,768]{2,1,0:T(8,128)} %get-tuple-element.806, s32[]{:T(128)S(6)} %select_n.262, s32[]{:T(128)S(6)} %select_n.265, f32[1,3,384,384]{3,2,1,0:T(8,128)S(1)} %slice.53, s32[]{:T(128)S(6)} %select_n.258), kind=kOutput, calls=%fused_computation.7.clone.1 | convolution fusion | flops 1359249408 | bytes 4128780 | tf_op jit(solution)/shard_map/while/body/dot_general | solution.py:28
  201.0 0.6 constant_dynamic-slice_fusion.9
  204.2 1.6 slice.53
  205.8 4.2 %convolution_add_fusion.9 = f32[768,384]{1,0:T(8,128)S(1)} fusion(f32[768,384]{1,0:T(8,128)S(1)} %get-tuple-element.787, f32[3,768,768]{2,1,0:T(8,128)} %get-tuple-element.806, s32[]{:T(128)S(6)} %select_n.262, s32[]{:T(128)S(6)} %select_n.265, f32[1,3,384,384]{3,2,1,0:T(8,128)S(1)} %slice.53, s32[]{:T(128)S(6)} %select_n.258), kind=kOutput, calls=%fused_computation.7.clone.1 | convolution fusion | flops 1359249408 | bytes 4128780 | tf_op jit(solution)/shard_map/while/body/dot_general | solution.py:28
  210.7 0.6 constant_dynamic-slice_fusion.9
  213.9 1.6 slice.53
  215.5 4.1 %convolution_add_fusion.9 = f32[768,384]{1,0:T(8,128)S(1)} fusion(f32[768,384]{1,0:T(8,128)S(1)} %get-tuple-element.787, f32[3,768,768]{2,1,0:T(8,128)} %get-tuple-element.806, s32[]{:T(128)S(6)} %select_n.262, s32[]{:T(128)S(6)} %select_n.265, f32[1,3,384,384]{3,2,1,0:T(8,128)S(1)} %slice.53, s32[]{:T(128)S(6)} %select_n.258), kind=kOutput, calls=%fused_computation.7.clone.1 | convolution fusion | flops 1359249408 | bytes 4128780 | tf_op jit(solution)/shard_map/while/body/dot_general | solution.py:28
  220.3 3.3 %maximum_add_fusion = f32[768,768]{1,0:T(8,128)} fusion(f32[768,384]{1,0:T(8,128)S(1)} %get-tuple-element.530, f32[768,384]{1,0:T(8,128)S(1)} %get-tuple-element.529, f32[384,768]{1,0:T(8,128)} %get-tuple-element.532, f32[384,768]{1,0:T(8,128)} %get-tuple-element.531), kind=kLoop, calls=%fused_computation.32 | loop fusion | flops 1769472 | bytes 7077888 | tf_op jit(solution)/shard_map/add | solution.py:89
Async XLA Ops:
  0.0 103.8 %collective-permute-start = (f32[768,768]{1,0:T(8,128)}, f32[768,768]{1,0:T(8,128)S(1)}, u32[]{:S(2)}, u32[]{:S(2)}) collective-permute-start(f32[768,768]{1,0:T(8,128)} %param.15), channel_id=1, source_target_pairs={{3,0},{0,1},{1,2},{2,3},{7,4},{4,5},{5,6},{6,7},{11,8},{8,9},{9,10... | collective-permute-start | bytes 7077896 | tf_op jit(solution)/shard_map/ppermute | solution.py:13
  1.6 102.2 %collective-permute-start.1 = (f32[768,768]{1,0:T(8,128)}, f32[768,768]{1,0:T(8,128)}, u32[]{:S(2)}, u32[]{:S(2)}) collective-permute-start(f32[768,768]{1,0:T(8,128)} %param.15), channel_id=1, source_target_pairs={{1,0},{2,1},{3,2},{0,3},{5,4},{6,5},{7,6},{4,7},{9,8},{10,9},{11,1... | collective-permute-start | bytes 7077896 | tf_op jit(solution)/shard_map/ppermute | solution.py:13
  2.0 101.7 %collective-permute-start.2 = (f32[768,768]{1,0:T(8,128)}, f32[768,768]{1,0:T(8,128)}, u32[]{:S(2)}, u32[]{:S(2)}) collective-permute-start(f32[768,768]{1,0:T(8,128)} %param.15), channel_id=1, source_target_pairs={{28,0},{0,4},{4,8},{8,12},{12,16},{16,20},{20,24},{24,28},{29,1},{... | collective-permute-start | bytes 7077896 | tf_op jit(solution)/shard_map/ppermute | solution.py:13
  2.0 101.7 %collective-permute-start.3 = (f32[768,768]{1,0:T(8,128)}, f32[768,768]{1,0:T(8,128)}, u32[]{:S(2)}, u32[]{:S(2)}) collective-permute-start(f32[768,768]{1,0:T(8,128)} %param.15), channel_id=1, source_target_pairs={{4,0},{8,4},{12,8},{16,12},{20,16},{24,20},{28,24},{0,28},{5,1},{9... | collective-permute-start | bytes 7077896 | tf_op jit(solution)/shard_map/ppermute | solution.py:13
  103.8 1.4 copy-start.1
  105.2 10.3 %copy-start = (f32[2,3,384,384]{3,2,1,0:T(8,128)S(1)}, f32[2,3,384,384]{3,2,1,0:T(8,128)}, u32[]{:S(2)}) copy-start(f32[2,3,384,384]{3,2,1,0:T(8,128)} %param.17) | copy-start | bytes 10616836
  105.2 10.4 %copy-start.2 = (s32[2,3]{1,0:T(2,128)S(1)}, s32[2,3]{1,0:T(2,128)}, u32[]{:S(2)}) copy-start(s32[2,3]{1,0:T(2,128)} %param.19) | copy-start | bytes 76
  143.7 27.0 %copy-start.3 = (s32[2,3]{1,0:T(2,128)S(1)}, s32[2,3]{1,0:T(2,128)}, u32[]{:S(2)}) copy-start(s32[2,3]{1,0:T(2,128)} %param.18) | copy-start | bytes 76
where the time goes:
time: 224 us
  waiting for transfers between devices  97.3 us (43%)
  matrix products  49.5 us (22%)
  loops' own time  38.9 us (17%)
  local copies, waits for them, and re-layouts  21.6 us (10%)
  other arithmetic  12.5 us (6%)
  starting transfers between devices  3.77 us (2%)
    ppermute x4, waiting for transfers between devices, from_behind(): return lax.ppermute(block, axis, route)  97.3 us
    dot_general x6, matrix products, alpha_accumulate(): jnp.dot(hblock, rows, precision=lax.Precision.HIGHEST, preferred_element_...  28.7 us
    another operation x2, loops' own time, alpha_section(): parts.append(lax.fori_loop(0, count[local], alpha_accumulate, start))  21.1 us
    dot_general x5, matrix products, beta_accumulate(): jnp.dot(columns, hblock, precision=lax.Precision.HIGHEST, preferred_eleme...  20.8 us
    another operation x2, loops' own time, beta_section(): parts.append(lax.fori_loop(0, count[local], beta_accumulate, start))  17.8 us
    another operation x1, other arithmetic, on_device(): jnp.stack([from_behind(coefficients, 'alpha', offset) if offset != 0 else...  9.21 us
    slice x5, local copies, waits for them, and re-layouts, beta_accumulate(): blocks[local]  7.97 us
  transfers between devices with their start and end apart: 4, of which 1 were waited for; matrix products, arithmetic and copies ran while one was open for 1% of the time, Pallas kernels for 0%

commit v1 on v0

v1 whole, which is shorter than its diff:
```python
import functools

import jax
import jax.numpy as jnp
from jax import lax
from jax.experimental import pallas as pl
from jax.experimental.pallas import tpu as pltpu
from jax.sharding import PartitionSpec as P

VMEM_LIMIT = 56 * 1024 * 1024


def halves(x):
    high = x.astype(jnp.bfloat16)
    low = (x - high.astype(jnp.float32)).astype(jnp.bfloat16)
    return high, low


def product(left, right):
    lh, ll = halves(left)
    rh, rl = halves(right)
    dot = functools.partial(jnp.dot, preferred_element_type=jnp.float32)
    return dot(lh, rh) + (dot(lh, rl) + dot(ll, rh))


def place(links, count, my_index, owners):
    per, listed = links.shape
    slot = (links - my_index * per + per) % (owners * per)
    return jnp.where(jnp.arange(listed)[None, :] < count[:, None], slot, -1).reshape(-1)


def add_rows(slots, base, at, tile, blocks, out, listed, group, per):
    def step(l, carry):
        slot = slots[at * listed + l]

        @pl.when((slot >= base) & (slot < base + per))
        def _():
            rows = pl.ds(pl.multiple_of((slot - base) * group, group), group)
            out[...] += product(blocks[0, l], tile[rows, :])

        return carry

    lax.fori_loop(0, listed, step, 0)


def add_columns(slots, offset, base, tile, blocks, out, listed, group, per):
    for c in range(per):

        def step(l, carry, c=c):
            slot = slots[offset + c * listed + l]

            @pl.when((slot >= base) & (slot < base + per))
            def _():
                columns = pl.ds(pl.multiple_of((slot - base) * group, group), group)
                out[:, c * group : (c + 1) * group] += product(tile[:, columns], blocks[c, l])

            return carry

        lax.fori_loop(0, listed, step, 0)


def own_kernel(slots, tile, tile_rows, ablocks, bblocks, out):
    per, listed, group, _ = bblocks.shape
    out[...] = jnp.zeros_like(out)
    add_rows(slots, per, pl.program_id(0), tile, ablocks, out, listed, group, per)
    add_columns(slots, per * listed, per, tile_rows, bblocks, out, listed, group, per)


def alpha_kernel(per, slots, running, behind, ahead, ablocks, out):
    _, listed, group, _ = ablocks.shape
    out[...] = running[...]
    for base, tile in ((0, behind), (2 * per, ahead)):
        add_rows(slots, base, pl.program_id(0), tile, ablocks, out, listed, group, per)


def beta_kernel(slots, running, behind, ahead, bblocks, out):
    per, listed, group, _ = bblocks.shape
    out[...] = running[...]
    for base, tile in ((0, behind), (2 * per, ahead)):
        add_columns(slots, per * listed, base, tile, bblocks, out, listed, group, per)


def call(kernel, grid, in_specs, out_spec, shape, flops, name, aliases):
    return pl.pallas_call(
        kernel,
        grid_spec=pltpu.PrefetchScalarGridSpec(
            num_scalar_prefetch=1, grid=(grid,), in_specs=in_specs, out_specs=out_spec
        ),
        out_shape=jax.ShapeDtypeStruct(shape, jnp.float32),
        input_output_aliases=aliases,
        compiler_params=pltpu.CompilerParams(vmem_limit_bytes=VMEM_LIMIT),
        cost_estimate=pl.CostEstimate(flops=flops, bytes_accessed=16 * 1024 * 1024, transcendentals=0),
        name=name,
    )


def on_device(c, bblocks, ablocks, blinks, alinks, bcount, acount):
    rows, columns = c.shape
    per, listed, group, _ = ablocks.shape
    na, nb = lax.axis_size("alpha"), lax.axis_size("beta")

    def shift(x, axis, n, by):
        return lax.ppermute(x, axis, [(i, (i + by) % n) for i in range(n)])

    b_behind = shift(c, "beta", nb, 1)
    b_ahead = shift(c, "beta", nb, -1)
    a_behind = shift(c, "alpha", na, 1)
    a_ahead = shift(c, "alpha", na, -1)

    slots = jnp.concatenate(
        [
            place(alinks, acount, lax.axis_index("alpha"), na),
            place(blinks, bcount, lax.axis_index("beta"), nb),
        ]
    )

    def whole(*shape):
        return pl.BlockSpec(shape, lambda i, s: (0,) * len(shape))

    def by_rows(n):
        return pl.BlockSpec((n, columns), lambda i, s: (i, 0))

    group_blocks = pl.BlockSpec((1, listed, group, group), lambda i, s: (i, 0, 0, 0))
    flops = 2 * rows * group * group * 3 * 3
    own = call(
        own_kernel, per,
        [whole(rows, columns), by_rows(group), group_blocks, whole(*bblocks.shape)],
        by_rows(group), c.shape, 2 * flops, "own_groups", {},
    )(slots, c, c, ablocks, bblocks)
    with_alpha = call(
        functools.partial(alpha_kernel, per), per,
        [by_rows(group), whole(rows, columns), whole(rows, columns), group_blocks],
        by_rows(group), c.shape, flops, "alpha_neighbours", {1: 0},
    )(slots, own, a_behind, a_ahead, ablocks)
    chunks = 4
    return call(
        beta_kernel, chunks,
        [by_rows(rows // chunks)] * 3 + [whole(*bblocks.shape)],
        by_rows(rows // chunks), c.shape, flops, "beta_neighbours", {1: 0},
    )(slots, with_alpha, b_behind, b_ahead, bblocks)


def solution(mesh):
    in_specs = (
        P("alpha", "beta"),
        P("beta", None, None, None),
        P("alpha", None, None, None),
        P("beta", None),
        P("alpha", None),
        P("beta"),
        P("alpha"),
    )
    return jax.shard_map(
        on_device, mesh=mesh, in_specs=in_specs, out_specs=P("alpha", "beta"), check_vma=False
    )
```

time: 224 us -> 121 us (0.54)
  the two profiles are of different devices: /device:TPU:22 before, /device:TPU:0 now
where the time goes in v1:
time: 121 us
  waiting for transfers between devices  82.9 us (69%)
  Pallas kernels  28.9 us (24%)
  starting transfers between devices  6.94 us (6%)
  other arithmetic  2.17 us (2%)
    ppermute x4, waiting for transfers between devices, shift(): return lax.ppermute(x, axis, [(i, (i + by) % n) for i in range(n)])  82.9 us
    pallas_call x1, Pallas kernels, on_device(): call(beta_kernel, chunks, [by_rows(rows // chunks)] * 3 + [whole(*bblocks...  12 us
    pallas_call x1, Pallas kernels, on_device(): call(functools.partial(alpha_kernel, per), per, [by_rows(group), whole(ro...  8.54 us
    pallas_call x1, Pallas kernels, on_device(): call(own_kernel, per, [whole(rows, columns), by_rows(group), group_blocks...  8.39 us
    ppermute x4, starting transfers between devices, shift(): return lax.ppermute(x, axis, [(i, (i + by) % n) for i in range(n)])  6.94 us
  transfers between devices with their start and end apart: 4, of which 3 were waited for; matrix products, arithmetic and copies ran while one was open for 2% of the time, Pallas kernels for 14%

profile of v1, /device:TPU:0, one launch (start us, length us, event | category | flops | bytes accessed | tf_op | source)
XLA Modules:
  0.0 121.1 jit_solution(12075151701815096887)
XLA Ops:
  0.0 3.3 %collective-permute-start.1 = (f32[768,768]{1,0:T(8,128)}, f32[768,768]{1,0:T(8,128)}, u32[]{:S(2)}, u32[]{:S(2)}) collective-permute-start(f32[768,768]{1,0:T(8,128)} %tile_rows.1), channel_id=1, source_target_pairs={{0,28},{4,0},{8,4},{12,8},{16,12},{20,16},{24,20},{28,24},{1,29},{... | collective-permute-start | bytes 7077896 | tf_op jit(solution)/shard_map/ppermute | solution.py:103
  3.3 0.0 collective-permute-start
  3.3 3.6 %collective-permute-start.3 = (f32[768,768]{1,0:T(8,128)}, f32[768,768]{1,0:T(8,128)S(1)}, u32[]{:S(2)}, u32[]{:S(2)}) collective-permute-start(f32[768,768]{1,0:T(8,128)} %tile_rows.1), channel_id=1, source_target_pairs={{0,3},{1,0},{2,1},{3,2},{4,7},{5,4},{6,5},{7,6},{8,11},{9,8},{10,9... | collective-permute-start | bytes 7077896 | tf_op jit(solution)/shard_map/ppermute | solution.py:103
  6.9 0.0 collective-permute-start.2
  6.9 0.8 compare_select_fusion.4
  7.7 0.1 reshape.9
  7.8 0.8 compare_select_fusion.5
  8.5 0.1 reshape.8
  8.6 0.7 pad_add_fusion.slots
  9.3 8.4 %own_groups.1.running = f32[768,768]{1,0:T(8,128)} custom-call(s32[12]{0:T(128)} %pad_add_fusion.slots, f32[768,768]{1,0:T(8,128)} %tile_rows.1, f32[768,768]{1,0:T(8,128)} %tile_rows.1, f32[2,3,384,384]{3,2,1,0:T(8,128)} %ablocks.3, f32[2,3,384,384]{3,2,1,0:T(8,128)} %bblocks.3), custom_call_target="tpu_custom_call" | custom-call | flops 4076863488 | bytes 16777216 | tf_op jit(solution)/shard_map/own_groups/pallas_call | solution.py:125
  17.7 36.7 %collective-permute-done.1.ahead = f32[768,768]{1,0:T(8,128)} collective-permute-done((f32[768,768]{1,0:T(8,128)}, f32[768,768]{1,0:T(8,128)}, u32[]{:S(2)}, u32[]{:S(2)}) %collective-permute-start.1) | collective-permute-done | bytes 2359328 | tf_op jit(solution)/shard_map/ppermute | solution.py:103
  54.3 2.0 %collective-permute-done.behind = f32[768,768]{1,0:T(8,128)} collective-permute-done((f32[768,768]{1,0:T(8,128)}, f32[768,768]{1,0:T(8,128)}, u32[]{:S(2)}, u32[]{:S(2)}) %collective-permute-start) | collective-permute-done | bytes 2359328 | tf_op jit(solution)/shard_map/ppermute | solution.py:103
  56.3 8.5 %alpha_neighbours.1.running = f32[768,768]{1,0:T(8,128)} custom-call(s32[12]{0:T(128)} %pad_add_fusion.slots, f32[768,768]{1,0:T(8,128)} %own_groups.1.running, f32[768,768]{1,0:T(8,128)} %collective-permute-done.behind, f32[768,768]{1,0:T(8,128)} %collective-permute-done.1.ahead, f32[2,3,384,384]{3,2,1,0:T(8,128)} %ablocks.3), custom_call_target="tpu_custom_call", output_to_operand_aliasing={{}: (1, {})} | custom-call | flops 2038431744 | bytes 16777216 | tf_op jit(solution)/shard_map/alpha_neighbours/pallas_call | solution.py:130
  64.9 0.0 collective-permute-done.3.ahead
  64.9 0.0 copy-start
  64.9 44.2 %collective-permute-done.2.behind = f32[768,768]{1,0:T(8,128)} collective-permute-done((f32[768,768]{1,0:T(8,128)}, f32[768,768]{1,0:T(8,128)}, u32[]{:S(2)}, u32[]{:S(2)}) %collective-permute-start.2) | collective-permute-done | bytes 2359328 | tf_op jit(solution)/shard_map/ppermute | solution.py:103
  109.1 0.0 copy-done
  109.1 12.0 %beta_neighbours.1 = f32[768,768]{1,0:T(8,128)} custom-call(s32[12]{0:T(128)} %pad_add_fusion.slots, f32[768,768]{1,0:T(8,128)} %alpha_neighbours.1.running, f32[768,768]{1,0:T(8,128)} %collective-permute-done.2.behind, f32[768,768]{1,0:T(8,128)} %copy-done, f32[2,3,384,384]{3,2,1,0:T(8,128)} %bblocks.3), custom_call_target="tpu_custom_call", output_to_operand_aliasing={{}: (1, {})} | custom-call | flops 2038431744 | bytes 16777216 | tf_op jit(solution)/shard_map/beta_neighbours/pallas_call | solution.py:136
Async XLA Ops:
  0.0 54.3 %collective-permute-start.1 = (f32[768,768]{1,0:T(8,128)}, f32[768,768]{1,0:T(8,128)}, u32[]{:S(2)}, u32[]{:S(2)}) collective-permute-start(f32[768,768]{1,0:T(8,128)} %tile_rows.1), channel_id=1, source_target_pairs={{0,28},{4,0},{8,4},{12,8},{16,12},{20,16},{24,20},{28,24},{1,29},{... | collective-permute-start | bytes 7077896 | tf_op jit(solution)/shard_map/ppermute | solution.py:103
  3.3 53.0 %collective-permute-start = (f32[768,768]{1,0:T(8,128)}, f32[768,768]{1,0:T(8,128)}, u32[]{:S(2)}, u32[]{:S(2)}) collective-permute-start(f32[768,768]{1,0:T(8,128)} %tile_rows.1), channel_id=1, source_target_pairs={{0,4},{4,8},{8,12},{12,16},{16,20},{20,24},{24,28},{28,0},{1,5},{5... | collective-permute-start | bytes 7077896 | tf_op jit(solution)/shard_map/ppermute | solution.py:103
  3.3 61.5 %collective-permute-start.3 = (f32[768,768]{1,0:T(8,128)}, f32[768,768]{1,0:T(8,128)S(1)}, u32[]{:S(2)}, u32[]{:S(2)}) collective-permute-start(f32[768,768]{1,0:T(8,128)} %tile_rows.1), channel_id=1, source_target_pairs={{0,3},{1,0},{2,1},{3,2},{4,7},{5,4},{6,5},{7,6},{8,11},{9,8},{10,9... | collective-permute-start | bytes 7077896 | tf_op jit(solution)/shard_map/ppermute | solution.py:103
  6.9 102.2 %collective-permute-start.2 = (f32[768,768]{1,0:T(8,128)}, f32[768,768]{1,0:T(8,128)}, u32[]{:S(2)}, u32[]{:S(2)}) collective-permute-start(f32[768,768]{1,0:T(8,128)} %tile_rows.1), channel_id=1, source_target_pairs={{0,1},{1,2},{2,3},{3,0},{4,5},{5,6},{6,7},{7,4},{8,9},{9,10},{10,1... | collective-permute-start | bytes 7077896 | tf_op jit(solution)/shard_map/ppermute | solution.py:103
  64.9 44.3 %copy-start = (f32[768,768]{1,0:T(8,128)}, f32[768,768]{1,0:T(8,128)S(1)}, u32[]{:S(2)}) copy-start(f32[768,768]{1,0:T(8,128)S(1)} %collective-permute-done.3.ahead) | copy-start | bytes 7077892
